TPU v7x, 512 devices: a whole 4x4x16 slice. The times are simulated.
512 devices in a mesh: ex: 64 (over z_hi, y, x), feat: 8 (over z_lo, core).
Axes of the slice: x: 4, y: 4, z: 16 (z_hi: 4, z_lo: 4; z = z_hi * 4 + z_lo), core: 2. Of those that a mesh axis runs over, the one named last changes fastest.
Arguments:
- grads: bfloat16 [8192, 8192], P('ex', 'feat')
Outputs:
- tiles: float32 [64, 1024, 1024], P('ex', 'feat')
All inputs are finite; a program needn't handle non-finite values.
Results may differ from a plain program's by a relative error of at most 0.0041.
Values may be sent and summed in bfloat16 or wider, within the bound.
A program may use at most 64 MiB of HBM per device.

v0:
```python
import math

import jax
import jax.numpy as jnp
from jax import lax
from jax.sharding import PartitionSpec as P


def partner(value, axis, distance):
    mask = 2**distance
    pairs = [(source, source ^ mask) for source in range(lax.axis_size(axis))]
    return lax.ppermute(value, axis, pairs)


def joined(upper, mine, other):
    return jnp.where(
        upper, jnp.concatenate([other, mine], axis=0), jnp.concatenate([mine, other], axis=0)
    )


def local(grads):
    rows, width = grads.shape
    index = lax.axis_index("ex")
    nbits = lax.axis_size("ex").bit_length() - 1
    low = min(nbits, 3)
    group = 1 << low
    nfeat = lax.axis_size("feat")
    fidx = lax.axis_index("feat")
    wide = grads.astype(jnp.float32)
    sumsq = lax.psum(jnp.sum(wide * wide, axis=1, keepdims=True), "feat")
    unit = (wide * lax.rsqrt(sumsq + 1e-06)).astype(jnp.bfloat16)
    row_panel = unit
    for bit in range(low):
        other = partner(row_panel, "ex", bit)
        row_panel = joined(index >> bit & 1 == 1, row_panel, other)
    col_panel = unit
    for bit in range(low, nbits):
        other = partner(col_panel, "ex", bit)
        col_panel = joined(index >> bit & 1 == 1, col_panel, other)
    share = row_panel.shape[0] // nfeat
    partial_value = jnp.einsum(
        "rf,cf->rc", row_panel, col_panel, preferred_element_type=jnp.float32
    )
    total = lax.psum(partial_value, "feat")
    summed = lax.dynamic_slice_in_dim(total, fidx * share, share, 0)
    scaled = summed * math.sqrt(width * nfeat)
    upper_id = index >> low
    lower_id = index & group - 1
    row_ids = upper_id * group * rows + fidx * share + jnp.arange(share, dtype=jnp.int32)
    col_pos = jnp.arange(col_panel.shape[0], dtype=jnp.int32)
    col_ids = (col_pos // rows * group + lower_id) * rows + col_pos % rows
    result = jnp.where(row_ids[:, None] == col_ids[None, :], jnp.float32(0.0), scaled)
    return result[None, :, :]


def solution(mesh):
    return jax.shard_map(
        local,
        mesh=mesh,
        in_specs=(P("ex", "feat"),),
        out_specs=P("ex", "feat", None),
        check_vma=False,
    )
```

profile of v0, /device:TPU:1, one launch (start us, length us, event | category | flops | bytes accessed | tf_op | source)
XLA Modules:
  0.0 320.6 jit_solution(9667417223201811142)
XLA Ops:
  6.5 0.0 all-reduce.2.cloned.1.call-start
  6.5 1.1 fusion.15
  7.6 19.8 %psum.14 = f32[128,1]{0,1:T(1,128)S(1)} all-reduce(f32[128,1]{0,1:T(1,128)S(1)} %bitcast.5), channel_id=1, replica_groups=mesh['ex'=64,'feat'=8] {'feat'}, use_global_device_ids=true, to_apply=%region_1.0 | all-reduce | flops 128 | bytes 1024 | tf_op jit(solution)/shard_map/psum | solution.py:30
  27.5 1.1 fusion.16
  28.5 1.9 collective-permute-start
  30.5 1.9 collective-permute-start.3
  32.4 5.3 %collective-permute-done = bf16[128,1024]{1,0:T(8,128)(2,1)S(1)} collective-permute-done((bf16[128,1024]{1,0:T(8,128)(2,1)S(1)}, bf16[128,1024]{1,0:T(8,128)(2,1)S(1)}, u32[]{:S(2)}, u32[]{:S(2)}) %collective-permute-start) | collective-permute-done | bytes 262176 | tf_op jit(solution)/shard_map/ppermute | solution.py:12
  37.7 3.3 %collective-permute-done.3 = bf16[128,1024]{1,0:T(8,128)(2,1)S(1)} collective-permute-done((bf16[128,1024]{1,0:T(8,128)(2,1)S(1)}, bf16[128,1024]{1,0:T(8,128)(2,1)S(1)}, u32[]{:S(2)}, u32[]{:S(2)}) %collective-permute-start.3) | collective-permute-done | bytes 262176 | tf_op jit(solution)/shard_map/ppermute | solution.py:12
  40.9 0.4 fusion.14
  41.3 4.0 %collective-permute-start.4 = (bf16[256,1024]{1,0:T(8,128)(2,1)S(1)}, bf16[256,1024]{1,0:T(8,128)(2,1)S(1)}, u32[]{:S(2)}, u32[]{:S(2)}) collective-permute-start(bf16[256,1024]{1,0:T(8,128)(2,1)S(1)} %get-tuple-element.5), channel_id=1, source_target_pairs={{0,128},{8,136},{16,144},{24,152},{32,160},{40,168},{48,176},{56,1... | collective-permute-start | bytes 1572872 | tf_op jit(solution)/shard_map/ppermute | solution.py:12
  45.3 4.4 %collective-permute-start.1 = (bf16[256,1024]{1,0:T(8,128)(2,1)S(1)}, bf16[256,1024]{1,0:T(8,128)(2,1)}, u32[]{:S(2)}, u32[]{:S(2)}) collective-permute-start(bf16[256,1024]{1,0:T(8,128)(2,1)S(1)} %get-tuple-element.6), channel_id=1, source_target_pairs={{0,16},{8,24},{16,0},{24,8},{32,48},{40,56},{48,32},{56,40},{64,80... | collective-permute-start | bytes 1572872 | tf_op jit(solution)/shard_map/ppermute | solution.py:12
  49.7 65.1 %collective-permute-done.4 = bf16[256,1024]{1,0:T(8,128)(2,1)S(1)} collective-permute-done((bf16[256,1024]{1,0:T(8,128)(2,1)S(1)}, bf16[256,1024]{1,0:T(8,128)(2,1)S(1)}, u32[]{:S(2)}, u32[]{:S(2)}) %collective-permute-start.4) | collective-permute-done | bytes 524320 | tf_op jit(solution)/shard_map/ppermute | solution.py:12
  114.7 0.5 maximum_select_fusion.5
  115.2 9.5 %collective-permute-start.5 = (bf16[512,1024]{1,0:T(8,128)(2,1)S(1)}, bf16[512,1024]{1,0:T(8,128)(2,1)}, u32[]{:S(2)}, u32[]{:S(2)}) collective-permute-start(bf16[512,1024]{1,0:T(8,128)(2,1)S(1)} %maximum_select_fusion.5), channel_id=1, source_target_pairs={{0,256},{8,264},{16,272},{24,280},{32,288},{40,296},{48,304},{56,3... | collective-permute-start | bytes 3145736 | tf_op jit(solution)/shard_map/ppermute | solution.py:12
  124.7 0.0 collective-permute-done.1
  124.7 1.6 maximum_select_fusion.4
  126.3 3.1 collective-permute-start.2
  129.4 36.1 %collective-permute-done.5 = bf16[512,1024]{1,0:T(8,128)(2,1)} collective-permute-done((bf16[512,1024]{1,0:T(8,128)(2,1)S(1)}, bf16[512,1024]{1,0:T(8,128)(2,1)}, u32[]{:S(2)}, u32[]{:S(2)}) %collective-permute-start.5) | collective-permute-done | bytes 1048608 | tf_op jit(solution)/shard_map/ppermute | solution.py:12
  165.5 0.0 collective-permute-done.2
  165.5 6.6 %fusion = f32[1024,1024]{1,0:T(8,128)} fusion(bf16[512,1024]{1,0:T(8,128)(2,1)S(1)} %maximum_select_fusion.4, bf16[512,1024]{1,0:T(8,128)(2,1)} %collective-permute-done.2, bf16[512,1024]{1,0:T(8,128)(2,1)S(1)} %maximum_select_fusion.5, bf16[512,1024]{1,0:T(8,128)(2,1)} %collective-permute-done.5, pred[]{:T(512)S(6)} %eq.39, pred[]{:T(512)S(6)} %eq.36), kind=kOutput, calls=%fused_computation.1 | convolution fusion | flops 2166358016 | bytes 8388610 | tf_op jit(solution)/shard_map/rf,cf->rc/dot_general | solution.py:41
  172.1 0.0 all-reduce.2.cloned.1.call-update
  172.1 139.7 %all-reduce.2.cloned.1.call-done = f32[1024,1024]{1,0:T(8,128)} async-done(((f32[1024,1024]{1,0:T(8,128)}), f32[1024,1024]{1,0:T(8,128)}) %all-reduce.2.cloned.1.call-update) | async-done | bytes 4194320 | tf_op jit(solution)/shard_map/psum | solution.py:44
  311.8 1.9 select_bitcast_fusion
  (3 shorter events, 0.0 us)
Async XLA Ops:
  6.5 305.3 %all-reduce.2.cloned.1.call-start = ((), (), s32[]{:S(2)}) async-start(), calls=%async_computation | async-start | bytes 8388608 | tf_op jit(solution)/shard_map/psum | solution.py:44
  28.5 9.1 %collective-permute-start = (bf16[128,1024]{1,0:T(8,128)(2,1)S(1)}, bf16[128,1024]{1,0:T(8,128)(2,1)S(1)}, u32[]{:S(2)}, u32[]{:S(2)}) collective-permute-start(bf16[128,1024]{1,0:T(8,128)(2,1)S(1)} %fusion.16), channel_id=1, source_target_pairs={{0,8},{8,0},{16,24},{24,16},{32,40},{40,32},{48,56},{56,48},{64,72... | collective-permute-start | bytes 786440 | tf_op jit(solution)/shard_map/ppermute | solution.py:12
  30.5 10.5 %collective-permute-start.3 = (bf16[128,1024]{1,0:T(8,128)(2,1)S(1)}, bf16[128,1024]{1,0:T(8,128)(2,1)S(1)}, u32[]{:S(2)}, u32[]{:S(2)}) collective-permute-start(bf16[128,1024]{1,0:T(8,128)(2,1)S(1)} %fusion.16), channel_id=1, source_target_pairs={{0,64},{8,72},{16,80},{24,88},{32,96},{40,104},{48,112},{56,120},{... | collective-permute-start | bytes 786440 | tf_op jit(solution)/shard_map/ppermute | solution.py:12
  41.3 73.4 %collective-permute-start.4 = (bf16[256,1024]{1,0:T(8,128)(2,1)S(1)}, bf16[256,1024]{1,0:T(8,128)(2,1)S(1)}, u32[]{:S(2)}, u32[]{:S(2)}) collective-permute-start(bf16[256,1024]{1,0:T(8,128)(2,1)S(1)} %get-tuple-element.5), channel_id=1, source_target_pairs={{0,128},{8,136},{16,144},{24,152},{32,160},{40,168},{48,176},{56,1... | collective-permute-start | bytes 1572872 | tf_op jit(solution)/shard_map/ppermute | solution.py:12
  45.3 79.4 %collective-permute-start.1 = (bf16[256,1024]{1,0:T(8,128)(2,1)S(1)}, bf16[256,1024]{1,0:T(8,128)(2,1)}, u32[]{:S(2)}, u32[]{:S(2)}) collective-permute-start(bf16[256,1024]{1,0:T(8,128)(2,1)S(1)} %get-tuple-element.6), channel_id=1, source_target_pairs={{0,16},{8,24},{16,0},{24,8},{32,48},{40,56},{48,32},{56,40},{64,80... | collective-permute-start | bytes 1572872 | tf_op jit(solution)/shard_map/ppermute | solution.py:12
  115.2 50.3 %collective-permute-start.5 = (bf16[512,1024]{1,0:T(8,128)(2,1)S(1)}, bf16[512,1024]{1,0:T(8,128)(2,1)}, u32[]{:S(2)}, u32[]{:S(2)}) collective-permute-start(bf16[512,1024]{1,0:T(8,128)(2,1)S(1)} %maximum_select_fusion.5), channel_id=1, source_target_pairs={{0,256},{8,264},{16,272},{24,280},{32,288},{40,296},{48,304},{56,3... | collective-permute-start | bytes 3145736 | tf_op jit(solution)/shard_map/ppermute | solution.py:12
  126.3 39.2 %collective-permute-start.2 = (bf16[512,1024]{1,0:T(8,128)(2,1)S(1)}, bf16[512,1024]{1,0:T(8,128)(2,1)}, u32[]{:S(2)}, u32[]{:S(2)}) collective-permute-start(bf16[512,1024]{1,0:T(8,128)(2,1)S(1)} %maximum_select_fusion.4), channel_id=1, source_target_pairs={{0,32},{8,40},{16,48},{24,56},{32,0},{40,8},{48,16},{56,24},{64,96... | collective-permute-start | bytes 3145736 | tf_op jit(solution)/shard_map/ppermute | solution.py:12
Sparse Core Ops, SparseCore 0:
  172.2 139.5 all-reduce.1
where the time goes:
time: 322 us; the launch traced here: 321 us
  waiting for transfers between devices  249 us (77%)
  starting transfers between devices  24.7 us (8%)
  blocking collectives  19.8 us (6%)
  between operations  13.5 us (4%)
  other arithmetic  6.59 us (2%)
  matrix products  6.56 us (2%)
    psum x1, waiting for transfers between devices, local(): total = lax.psum(partial_value, 'feat')  140 us
    ppermute x6, waiting for transfers between devices, partner(): return lax.ppermute(value, axis, pairs)  110 us
    ppermute x6, starting transfers between devices, partner(): return lax.ppermute(value, axis, pairs)  24.7 us
    psum x1, blocking collectives, local(): sumsq = lax.psum(jnp.sum(wide * wide, axis=1, keepdims=True), 'feat')  19.8 us
    dot_general x1, matrix products, local(): jnp.einsum('rf,cf->rc', row_panel, col_panel, preferred_element_type=jnp....  6.56 us
  transfers between devices with their start and end apart: 7, of which 5 were waited for; matrix products, arithmetic and copies ran while one was open for 1% of the time, Pallas kernels for 0%

commit v1 on v0

v1 whole, which is shorter than its diff:
```python
import functools
import math

import jax
import jax.numpy as jnp
from jax import lax
from jax.experimental import pallas as pl
from jax.experimental.pallas import tpu as pltpu
from jax.sharding import PartitionSpec as P

MESH = pl.DeviceIdType.MESH
NZ = 16
ROWS = 128
WIDTH = 1024
CHUNKS = 4
PIECE = ROWS // CHUNKS
RING = CHUNKS * 15 // 2
RUN_RING = True
RUN_XY = True
RUN_MATH = True


def kernel(
    g_ref, out_ref, cols, rows, acc, colsq, rowsq, sqsend, sqrecv, half, swap_out, swap_in,
    load_sem, ring_send, ring_recv, xy_send, xy_recv, tail_send, tail_recv,
):
    ex = lax.axis_index("ex")
    feat = lax.axis_index("feat")
    h, y, x = ex // 16, ex // 4 % 4, ex % 4
    l, c = feat // 2, feat % 2
    z = h * 4 + l
    big_y = y // 2
    dx = (x - l % 2 * 2 + 4) % 4
    dy = (y - l // 2 + 4) % 4

    def device(zz, yy, xx, cc):
        return (zz // 4 * 16 + yy * 4 + xx, zz % 4 * 2 + cc)

    zu, zd = device((z + 1) % NZ, y, x, c), device((z + NZ - 1) % NZ, y, x, c)
    xu, xd = device(z, y, (x + 1) % 4, c), device(z, y, (x + 3) % 4, c)
    yu, yd = device(z, (y + 1) % 4, x, c), device(z, (y + 3) % 4, x, c)
    opposite = device(z, (y + 2) % 4, x, c)
    sibling = device(z, y, x, 1 - c)

    load = pltpu.make_async_copy(g_ref, cols.at[z], load_sem.at[0])
    load.start()
    barrier = pltpu.get_barrier_semaphore()
    for to in (zu, zd, xu, xd, yu, yd, opposite, sibling):
        pl.semaphore_signal(barrier, inc=1, device_id=to, device_id_type=MESH)
    pl.semaphore_wait(barrier, 8)
    load.wait()

    sent = []

    def remote(src, dst, send, recv, to):
        return pltpu.make_async_remote_copy(
            src_ref=src, dst_ref=dst, send_sem=send, recv_sem=recv, device_id=to,
            device_id_type=MESH,
        )

    def ring_copy(way, n):
        far, j = n // CHUNKS, n % CHUNKS
        if way == 1:
            j = CHUNKS - 1 - j
        owner = (z - far + NZ) % NZ if way == 0 else (z + far) % NZ
        ref = cols.at[owner, pl.ds(j * PIECE, PIECE)]
        return remote(ref, ref, ring_send.at[way, n], ring_recv.at[way, n], zu if way == 0 else zd)

    def ring_arrival(way, n):
        far, j = n // CHUNKS + 1, n % CHUNKS
        if way == 1:
            j = CHUNKS - 1 - j
        owner = (z - far + NZ) % NZ if way == 0 else (z + far) % NZ
        ref = cols.at[owner, pl.ds(j * PIECE, PIECE)]
        return remote(ref, ref, ring_send.at[way, n], ring_recv.at[way, n], zu if way == 0 else zd)

    def ring_start(n):
        for way in range(2):
            ring_copy(way, n).start()

    def ring_round(n):
        for way in range(2):
            ring_arrival(way, n).wait_recv()
            if n + CHUNKS < RING:
                ring_copy(way, n + CHUNKS).start()

    low, high = pl.ds(0, 64), pl.ds(64, 64)
    source = (dx < 2) & (dy % 2 == 0)
    own_y = dy // 2

    def slice_of(k):
        return (l, l + 1 - l % 2 * 2, (l + 2) % 4, 3 - l)[k]

    def a_at(k, yy, i):
        return rows.at[slice_of(k), 2 * yy + i]

    def a_pair(k, yy):
        return rows.at[slice_of(k), pl.ds(2 * yy, 2)]

    def b_at(k, yy, i):
        return rows.at[slice_of(k), 4 + 2 * i + yy]

    def b_pair(k, i):
        return rows.at[slice_of(k), pl.ds(4 + 2 * i, 2)]

    def go(k, sem, recv, src, dst, to, cond):
        remote(src, dst, xy_send.at[k, sem], xy_recv.at[k, recv], to).start()
        sent.append((cond, k, sem, len(src.shape) == 3))

    def await_(k, recv, dst):
        remote(dst, dst, xy_send.at[k, 0], xy_recv.at[k, recv], xu).wait_recv()

    even, left = dy % 2 == 0, dx < 2
    odd, right = dy % 2 == 1, dx >= 2
    even_left, even_right, odd_left = even & left, even & right, odd & left
    even_2, even_3 = even & (dx == 2), even & (dx == 3)
    dx_2, dx_3, dy_1, dy_3 = dx == 2, dx == 3, dy == 1, dy == 3

    def step1(k):
        @pl.when(source)
        def _():
            shard = h * 4 + slice_of(k)
            first = pltpu.make_async_copy(
                cols.at[shard, low], a_at(k, own_y, dx), load_sem.at[1])
            second = pltpu.make_async_copy(
                cols.at[shard, high], b_at(k, own_y, dx), load_sem.at[2])
            first.start()
            second.start()
            go(k, 0, 0, cols.at[shard, low], a_at(k, own_y, dx), xu, source)
            go(k, 2, 2 + own_y, cols.at[shard, high], b_at(k, own_y, dx), yu, source)
            go(k, 1, 0, cols.at[shard, low], a_at(k, own_y, dx), xd, source)
            go(k, 3, 2 + own_y, cols.at[shard, high], b_at(k, own_y, dx), yd, source)
            first.wait()
            second.wait()

    def a3(k, cond):
        go(k, 6, 5 + own_y, a_pair(k, own_y), a_pair(k, own_y), yu, cond)
        go(k, 7, 5 + own_y, a_pair(k, own_y), a_pair(k, own_y), yd, cond)

    def b3(k, cond):
        go(k, 10, 9, b_pair(k, dx), b_pair(k, dx), xu, cond)
        go(k, 11, 9, b_pair(k, dx), b_pair(k, dx), xd, cond)

    def step2(k):
        @pl.when(even)
        def _():
            await_(k, 0, a_at(k, own_y, (dx + 1) % 2))

            @pl.when(dx_2)
            def _():
                go(k, 4, 1, a_at(k, own_y, 1), a_at(k, own_y, 1), xu, even_2)

            @pl.when(dx_3)
            def _():
                go(k, 4, 1, a_at(k, own_y, 0), a_at(k, own_y, 0), xd, even_3)

            @pl.when(left)
            def _():
                a3(k, even_left)

        @pl.when(odd_left)
        def _():
            await_(k, 2, b_at(k, 0, dx))
            await_(k, 3, b_at(k, 1, dx))
            go(k, 5, 4, b_at(k, own_y, dx), b_at(k, own_y, dx), yu, odd_left)
            b3(k, odd_left)

    def step3(k):
        @pl.when(even_right)
        def _():
            await_(k, 1, a_at(k, own_y, dx % 2))
            a3(k, even_right)

        @pl.when(even_left)
        def _():
            await_(k, 4, b_at(k, 1 - own_y, dx))
            b3(k, even_left)

    def step4(k):
        @pl.when(odd)
        def _():
            await_(k, 5, a_pair(k, 0))
            await_(k, 6, a_pair(k, 1))

            @pl.when(dy_1)
            def _():
                go(k, 8, 7, a_at(k, 0, 0), a_at(k, 0, 0), yu, dy_1)
                go(k, 9, 7, a_at(k, 1, 0), a_at(k, 1, 0), yd, dy_1)

            @pl.when(dy_3)
            def _():
                go(k, 8, 8, a_at(k, 0, 1), a_at(k, 0, 1), yd, dy_3)
                go(k, 9, 8, a_at(k, 1, 1), a_at(k, 1, 1), yu, dy_3)

        await_(k, 9, b_pair(k, (dx + 1) % 2))

        @pl.when(dx_2)
        def _():
            go(k, 12, 10, b_pair(k, 1), b_pair(k, 1), xu, dx_2)

        @pl.when(dx_3)
        def _():
            go(k, 12, 10, b_pair(k, 0), b_pair(k, 0), xd, dx_3)

    def step5(k):
        @pl.when(even)
        def _():
            await_(k, 7, a_at(k, 1 - own_y, 0))
            await_(k, 8, a_at(k, 1 - own_y, 1))

        @pl.when(right)
        def _():
            await_(k, 10, b_pair(k, dx % 2))

    def squares(block):
        wide = block.astype(jnp.float32)
        wide = wide * wide
        total = wide[:, :128]
        for piece in range(1, WIDTH // 128):
            total = total + wide[:, piece * 128:piece * 128 + 128]
        return total

    def multiply(shard):
        hh, ll = shard // 4, shard % 4
        block = cols[shard]
        acc[hh] += lax.dot_general(
            rows[ll].reshape(512, WIDTH), block, (((1,), (1,)), ((), ())),
            preferred_element_type=jnp.float32,
        )
        colsq[hh] += squares(block)

    def row_squares():
        for ll in range(4):
            for part in range(8):
                rowsq[part] += squares(rows[ll, part])

    if RUN_MATH:
        acc[...] = jnp.zeros_like(acc)
        colsq[...] = jnp.zeros_like(colsq)
        rowsq[...] = jnp.zeros_like(rowsq)

    plan = {}
    if RUN_XY:
        for k in range(4):
            plan.setdefault(2 * k, []).append((step1, k))
            plan.setdefault(3 * k + 1, []).append((step2, k))
            plan.setdefault(3 * k + 2, []).append((step3, k))
            plan.setdefault(3 * k + 4, []).append((step4, k))
            plan.setdefault(99, []).append((step5, k))

    if RUN_RING:
        for n in range(CHUNKS):
            ring_start(n)
    unit = CHUNKS // 2
    for tick in range(16):
        for step, k in plan.get(tick, ()):
            step(k)
        if RUN_RING and tick < 15:
            for n in range(tick * unit, (tick + 1) * unit):
                ring_round(n)
    for step, k in plan.get(99, ()):
        step(k)

    if RUN_MATH:
        row_squares()

        def body(s, carry):
            multiply(s)
            return carry

        lax.fori_loop(0, NZ, body, 0)

        eye = lax.broadcasted_iota(jnp.int32, (128, 128), 0) == lax.broadcasted_iota(
            jnp.int32, (128, 128), 1)

        def to_lanes(column):
            return jnp.sum(jnp.where(eye, column, 0.0), axis=0, keepdims=True)

        def to_rows(lanes):
            return jnp.sum(jnp.where(eye, lanes, 0.0), axis=1, keepdims=True)

        for hh in range(4):
            sqsend[hh:hh + 1] = to_lanes(jnp.sum(colsq[hh], axis=1, keepdims=True))
        for yy in range(2):
            for i in range(2):
                both = jnp.concatenate([rowsq[2 * yy + i], rowsq[4 + 2 * i + yy]], axis=0)
                sqsend[4 + 2 * yy + i:5 + 2 * yy + i] = to_lanes(
                    jnp.sum(both, axis=1, keepdims=True))
        squares_swap = remote(sqsend, sqrecv, tail_send.at[0], tail_recv.at[0], sibling)
        squares_swap.start()

        other = 1 - c
        for yy in range(2):
            for hh in range(4):
                swap_out[yy, hh, :64] = acc[hh, pl.ds(pl.multiple_of((2 * yy + other) * 64, 64), 64)]
                swap_out[yy, hh, 64:] = acc[
                    hh, pl.ds(pl.multiple_of((4 + 2 * other + yy) * 64, 64), 64)]
        halves = remote(swap_out, swap_in, tail_send.at[1], tail_recv.at[1], sibling)
        halves.start()
        squares_swap.wait()
        inverse = lax.rsqrt(sqsend[...] + sqrecv[...] + 1e-6)
        halves.wait()

        def result(yy, hh):
            row_scale = to_rows(
                jnp.where(c == 0, inverse[4 + 2 * yy:5 + 2 * yy], inverse[5 + 2 * yy:6 + 2 * yy]))
            col_scale = inverse[hh:hh + 1]
            top = acc[hh, pl.ds(pl.multiple_of((2 * yy + c) * 64, 64), 64)]
            bottom = acc[hh, pl.ds(pl.multiple_of((4 + 2 * c + yy) * 64, 64), 64)]
            raw = jnp.concatenate([top, bottom], axis=0) + swap_in[yy, hh]
            value = raw * row_scale * (col_scale * math.sqrt(8192.0))
            value = jnp.where((row_scale > 0.0) & (col_scale > 0.0), value, 0.0)
            same = (hh == h) & (yy == big_y) & (2 * l + c == ex % 8)
            return jnp.where(eye & same, 0.0, value)

        for hh in range(4):
            for yy in range(2):
                @pl.when(yy != big_y)
                def _():
                    half[0, hh] = result(yy, hh).astype(jnp.bfloat16)
        across = remote(half.at[0], half.at[1], tail_send.at[2], tail_recv.at[2], opposite)
        across.start()
        for hh in range(4):
            for yy in range(2):
                @pl.when(yy == big_y)
                def _():
                    out_ref[0, :, (2 * hh + yy) * 128:(2 * hh + yy + 1) * 128] = result(yy, hh)
        across.wait()
        for hh in range(4):
            for yy in range(2):
                @pl.when(yy != big_y)
                def _():
                    out_ref[0, :, (2 * hh + yy) * 128:(2 * hh + yy + 1) * 128] = half[1, hh].astype(
                        jnp.float32)
    else:
        out_ref[...] = jnp.zeros_like(out_ref)

    if RUN_RING:
        for n in range(RING):
            for way in range(2):
                ring_copy(way, n).wait_send()
    for cond, k, sem, pair in sent:
        @pl.when(cond)
        def _():
            ref = rows.at[0, pl.ds(0, 2)] if pair else rows.at[0, 0]
            remote(ref, ref, xy_send.at[k, sem], xy_recv.at[k, 0], xu).wait_send()


def local(grads):
    return pl.pallas_call(
        kernel,
        out_shape=jax.ShapeDtypeStruct((1, 128, 1024), jnp.float32),
        in_specs=[pl.BlockSpec(memory_space=pl.ANY)],
        out_specs=pl.BlockSpec(memory_space=pltpu.VMEM),
        scratch_shapes=[
            pltpu.VMEM((NZ, ROWS, WIDTH), jnp.bfloat16),
            pltpu.VMEM((4, 8, 64, WIDTH), jnp.bfloat16),
            pltpu.VMEM((4, 512, 128), jnp.float32),
            pltpu.VMEM((4, 128, 128), jnp.float32),
            pltpu.VMEM((8, 64, 128), jnp.float32),
            pltpu.VMEM((8, 128), jnp.float32),
            pltpu.VMEM((8, 128), jnp.float32),
            pltpu.VMEM((2, 4, 128, 128), jnp.bfloat16),
            pltpu.VMEM((2, 4, 128, 128), jnp.float32),
            pltpu.VMEM((2, 4, 128, 128), jnp.float32),
            pltpu.SemaphoreType.DMA((3,)),
            pltpu.SemaphoreType.DMA((2, RING)),
            pltpu.SemaphoreType.DMA((2, RING)),
            pltpu.SemaphoreType.DMA((4, 13)),
            pltpu.SemaphoreType.DMA((4, 11)),
            pltpu.SemaphoreType.DMA((3,)),
            pltpu.SemaphoreType.DMA((3,)),
        ],
        compiler_params=pltpu.CompilerParams(
            collective_id=0, has_side_effects=True, vmem_limit_bytes=32 * 1024 * 1024
        ),
        cost_estimate=pl.CostEstimate(
            flops=2 * 512 * 512 * 4096, bytes_accessed=1 << 20, transcendentals=0),
    )(grads)


def solution(mesh):
    return jax.shard_map(
        local,
        mesh=mesh,
        in_specs=(P("ex", "feat"),),
        out_specs=P("ex", "feat", None),
        check_vma=False,
    )
```

time: 322 us -> 92.4 us (0.29)
  the two profiles are of different devices: /device:TPU:1 before, /device:TPU:40 now
where the time goes in v1:
time: 92.4 us; the launch traced here: 92.3 us
  Pallas kernels  90.5 us (98%)
  local copies, waits for them, and re-layouts  1.75 us (2%)
    pallas_call x1, Pallas kernels, local(): pl.pallas_call(kernel, out_shape=jax.ShapeDtypeStruct((1, 128, 1024), jnp...  90.5 us

profile of v1, /device:TPU:40, one launch (start us, length us, event | category | flops | bytes accessed | tf_op | source)
XLA Modules:
  0.0 92.3 jit_solution(8267449513356092339)
XLA Ops:
  0.0 0.0 copy-start
  0.0 0.9 %copy-done = bf16[128,1024]{1,0:T(8,128)(2,1)S(1)} copy-done((bf16[128,1024]{1,0:T(8,128)(2,1)S(1)}, bf16[128,1024]{1,0:T(8,128)(2,1)}, u32[]{:S(2)}) %copy-start) | copy-done | bytes 262168
  1.0 90.5 %shard_map.17 = f32[1,128,1024]{2,1,0:T(8,128)S(1)} custom-call(bf16[128,1024]{1,0:T(8,128)(2,1)S(1)} %copy-done), custom_call_target="tpu_custom_call" | custom-call | flops 2147483648 | bytes 1048576 | tf_op jit(solution)/shard_map/pallas_call | solution.py:350
  91.5 0.8 copy.3
Async XLA Ops:
  0.0 0.9 %copy-start = (bf16[128,1024]{1,0:T(8,128)(2,1)S(1)}, bf16[128,1024]{1,0:T(8,128)(2,1)}, u32[]{:S(2)}) copy-start(bf16[128,1024]{1,0:T(8,128)(2,1)} %g_ref.1) | copy-start | bytes 786436

commit v2 on v0

v2 whole, which is shorter than its diff:
```python
import math

import jax
import jax.numpy as jnp
from jax import lax
from jax.experimental import pallas as pl
from jax.experimental.pallas import tpu as pltpu
from jax.sharding import PartitionSpec as P

MESH = pl.DeviceIdType.MESH
NZ = 16
ROWS = 128
WIDTH = 1024
CHUNKS = 4
PIECE = 32
RING = 30
RUN_RING = True
RUN_XY = True
RUN_MATH = True
P_TICKS = (16, 20, 21, 24, 25)
SQ_TICKS = (13, 17, 22, 26)
EVENTS = (
    (51561376, 76382242, 52086690, 75858976, 42126276, 85805126, 42651590, 85281860, 67453349, 68995716, 67978663,
     68472454, 68520385, 67945088, 69045699, 67421826),
    (1495976, 11046020, 2021290, 10520710, 449484, 20464768, 974798, 19939458, 1575341, 17056896, 1052079,
     67387522, 524745, 9735300, 1483, 68454534),
    (890882, 397000, 367616, 920266, 1921030, 1443500, 1397764, 1966766, 69554183, 36756227, 70079493, 37281347,
     70621187, 35705607, 71146497, 36230695),
    (96952326, 20519211, 97477636, 37263657, 98019330, 11080015, 98544640, 36196685, 114558466, 35654927,
     115081728, 36178189, 121900550, 36701451, 122423812, 37224713),
    (2625037, 71066629, 2099727, 70541319, 3671561, 70036481, 3146251, 69511171, 3939340, 70029866, 3414030,
     19796520, 2888712, 71064142, 2363402, 12458572),
    (115349204, 80483024, 115872470, 79959762, 124788400, 89922228, 125311666, 89398966, 2761392, 73214069,
     2238130, 72690807, 3812052, 72163441, 3288790, 71640179),
    (5512569, 15248532, 6035835, 14756948, 4461949, 24667280, 4985215, 24192048, 5470731, 13180942, 5996041,
     12657676, 4436495, 22620170, 4961805, 22096904),
    (57680911, 56765965, 58204173, 57289231, 48245771, 49423881, 48769033, 49947147, 48246294, 32908881, 48769556,
     33335057, 57681426, 31862325, 58204688, 32272149),
    (7613459, 40903483, 8136721, 24127289, 6562839, 39856991, 7086101, 14692189, 4990233, 5914268, 4464923,
     5388958, 6040861, 4863640, 5515551, 4338330),
    (7091223, 5652062, 6565909, 6175390, 8141843, 4601402, 7616529, 5124762, 8141852, 23360664, 7616542, 73691290,
     7091224, 16039068, 6565914, 74758302),
    (15902, 14873, 14876, 15899, 13850, 12829, 12824, 13855, 13850, 15643, 12824, 14427, 15902, 13599, 14876, 12351),
)
DONE = (
    (101462146, 50864128, 101462146, 50864128, 101462146, 50864128, 101462146, 50864128, 17043456, 0, 17043456, 0,
     17043456, 0, 17043456, 0),
    (238068167, 203718981, 238068167, 203718981, 238068167, 203718981, 238068167, 203718981, 136069315, 152846531,
     136069315, 152846531, 136069315, 152846531, 136069315, 152846531),
    (391464015, 340857869, 391464015, 340857869, 391464015, 340857869, 391464015, 340857869, 289469195, 305984203,
     289469195, 305984203, 289469195, 305984203, 289469195, 305984203),
    (494253720, 510772760, 494253720, 510772760, 494253720, 510772760, 494253720, 510772760, 459638100, 459634003,
     459638100, 459634003, 459638100, 459634003, 459638100, 459634003),
    (545392607, 545388510, 545392607, 545388510, 545392607, 545388510, 545392607, 545388510, 545384348, 545388509,
     545384348, 545388509, 545384348, 545388509, 545384348, 545388509),
    (133152, 133152, 133152, 133152, 133152, 133152, 133152, 133152, 133152, 133152, 133152, 133152, 133152,
     133152, 133152, 133152),
)


def kernel(
    g_ref, out_ref, cols, rows, acc, colsq, rowsq, sq_out, sq_in, swap_in, half_out, half_in,
    load_sem, ring_send, ring_recv, xy_send, xy_recv, tail_send, tail_recv,
):
    ex = lax.axis_index("ex")
    feat = lax.axis_index("feat")
    h, y, x = ex // 16, ex // 4 % 4, ex % 4
    l, c = feat // 2, feat % 2
    z = h * 4 + l
    big_y = y // 2
    dx = (x - l % 2 * 2 + 4) % 4
    dy = (y - l // 2 + 4) % 4

    def device(zz, yy, xx, cc):
        return (zz // 4 * 16 + yy * 4 + xx, zz % 4 * 2 + cc)

    z_up, z_down = device((z + 1) % NZ, y, x, c), device((z + NZ - 1) % NZ, y, x, c)
    plane = (
        device(z, y, (x + 1) % 4, c), device(z, y, (x + 3) % 4, c),
        device(z, (y + 1) % 4, x, c), device(z, (y + 3) % 4, x, c),
    )
    opposite = device(z, (y + 2) % 4, x, c)
    sibling = device(z, y, x, 1 - c)

    def remote(src, dst, send, recv, to):
        return pltpu.make_async_remote_copy(
            src_ref=src, dst_ref=dst, send_sem=send, recv_sem=recv, device_id=to,
            device_id_type=MESH,
        )

    load = pltpu.make_async_copy(g_ref, cols.at[z], load_sem)
    load.start()
    barrier = pltpu.get_barrier_semaphore()
    for to in (z_up, z_down, *plane, opposite, sibling):
        pl.semaphore_signal(barrier, inc=1, device_id=to, device_id_type=MESH)
    acc[...] = jnp.zeros_like(acc)
    colsq[...] = jnp.zeros_like(colsq)
    load.wait()
    pl.semaphore_wait(barrier, 8)

    def ring_copy(way, n, far):
        j = n % CHUNKS if way == 0 else CHUNKS - 1 - n % CHUNKS
        owner = (z - far + NZ) % NZ if way == 0 else (z + far) % NZ
        ref = cols.at[owner, j]
        to = z_up if way == 0 else z_down
        return remote(ref, ref, ring_send.at[way, n], ring_recv.at[way, n], to)

    def ring_start(n):
        for way in range(2):
            ring_copy(way, n, n // CHUNKS).start()

    def ring_round(n):
        for way in range(2):
            ring_copy(way, n, n // CHUNKS + 1).wait_recv()
            if n + CHUNKS < RING:
                ring_copy(way, n + CHUNKS, n // CHUNKS + 1).start()

    def ring_sent(n):
        for way in range(2):
            ring_copy(way, n, 0).wait_send()

    place = dx * 4 + dy
    source = (dx < 2) & (dy % 2 == 0)

    def here(table):
        value = jnp.int32(table[0])
        for index, entry in enumerate(table[1:], 1):
            value = jnp.where(place == index, jnp.int32(entry), value)
        return value

    events = [here(table) for table in EVENTS]
    done = [here(table) for table in DONE]
    handled = [jnp.int32(0)] + [done[n // 5] // 64 ** (n % 5) % 64 for n in range(28)]

    def slice_of(k):
        return (l // 2 + k // 2) % 2 * 2 + (l + k) % 2

    def own_copy(k, part):
        q = 2 * (2 * dx + dy // 2) + part
        return pltpu.make_async_copy(
            cols.at[h * 4 + slice_of(k), pl.ds(2 * part, 2)],
            rows.at[slice_of(k), pl.ds(2 * q, 2)], xy_recv.at[k, q],
        )

    def set_out(k):
        @pl.when(source)
        def _():
            for part in range(2):
                own_copy(k, part).start()

    def decoded(e):
        third = e // 3
        word = events[0]
        for index in range(1, len(events)):
            word = jnp.where(third == index, events[index], word)
        digit = jnp.right_shift(word, (e - third * 3) * 9)
        return digit // 8 % 4, digit % 8, [digit // (32 * 2**d) % 2 == 1 for d in range(4)]

    def onward(k, q, d):
        ref = rows.at[slice_of(k), pl.ds(2 * q, 2)]
        return remote(ref, ref, xy_send.at[k, 4 * q + d], xy_recv.at[k, q], plane[d])

    def take(e, carry):
        k, q, goes = decoded(e)
        onward(k, q, 0).wait_recv()
        for d in range(4):
            pl.when(goes[d])(onward(k, q, d).start)
        return carry

    def take_until(n):
        lax.fori_loop(handled[n], handled[n + 1], take, 0)

    def xy_sent():
        def body(e, carry):
            k, q, goes = decoded(e)
            for d in range(4):
                pl.when(goes[d])(onward(k, q, d).wait_send)
            return carry

        lax.fori_loop(0, 32, body, 0)

    def squares(block):
        wide = block.astype(jnp.float32)
        wide = wide * wide
        total = wide[:, :128]
        for part in range(1, WIDTH // 128):
            total = total + wide[:, part * 128:part * 128 + 128]
        return total

    def cube(b):
        return (h + b + b // 2 - b // 3 * 2) % 4

    def multiply(b, k):
        ll = slice_of(k)
        block = cols[cube(b) * 4 + ll].reshape(ROWS, WIDTH)
        product = lax.dot_general(
            rows[ll].reshape(4 * ROWS, WIDTH), block, (((1,), (1,)), ((), ())),
            preferred_element_type=jnp.float32,
        )
        acc[b] += product.reshape(4, ROWS, 128)
        colsq[b] += squares(block)

    def multiply_all(k, blocks):
        def body(i, carry):
            b = blocks[0]
            for index in range(1, len(blocks)):
                b = jnp.where(i == index, blocks[index], b)
            multiply(b % 4, k)
            return carry

        lax.fori_loop(0, len(blocks), body, 0)

    def row_squares(k):
        ll = slice_of(k)

        def body(i, carry):
            total = squares(rows[ll, pl.ds(4 * i, 4)].reshape(ROWS, WIDTH))
            if k:
                total = total + rowsq[i]
            rowsq[i] = total
            return carry

        lax.fori_loop(0, 4, body, 0)

    eye = lax.broadcasted_iota(jnp.int32, (128, 128), 0) == lax.broadcasted_iota(
        jnp.int32, (128, 128), 1)

    def to_lanes(folded):
        column = jnp.sum(folded, axis=1, keepdims=True)
        return jnp.sum(jnp.where(eye, column, 0.0), axis=0, keepdims=True)

    def to_rows(lanes):
        return jnp.sum(jnp.where(eye, lanes, 0.0), axis=1, keepdims=True)

    last = jnp.where(l == 0, 1, jnp.where(l == 3, 2, 3))

    far = jnp.where(l < 2, 1, 2)
    plan = {
        P_TICKS[0]: lambda: multiply_all(0, (0, 1, 2)),
        P_TICKS[1]: lambda: multiply_all(1, (0, 1, 2)),
        P_TICKS[2]: lambda: multiply_all(2, (0, 3 - far)),
        P_TICKS[3]: lambda: multiply_all(2, (far, 3)),
        P_TICKS[4]: lambda: multiply_all(3, (last + 1, last + 2, last + 3)),
    }
    if RUN_RING:
        for n in range(CHUNKS):
            ring_start(n)
    for tick in range(28):
        if RUN_XY:
            if tick % CHUNKS == 0 and tick < 4 * CHUNKS:
                set_out(tick // CHUNKS)
            take_until(tick)
        if RUN_MATH:
            if tick in SQ_TICKS:
                row_squares(SQ_TICKS.index(tick))
            if tick in plan:
                plan[tick]()
        if RUN_RING:
            ring_round(tick)

    other = 1 - c
    if RUN_MATH:
        multiply(3, 1)
        multiply(last, 3)
        for b in range(3):
            sq_out[0, b:b + 1] = to_lanes(colsq[b])
        for p in range(4):
            sq_out[0, 4 + p:5 + p] = to_lanes(rowsq[p])
        swaps = [
            remote(sq_out.at[0], sq_in.at[0], tail_send.at[0], tail_recv.at[0], sibling),
            remote(
                acc.at[pl.ds(0, 3), pl.ds(2 * other, 2)], swap_in.at[pl.ds(0, 3)], tail_send.at[1],
                tail_recv.at[1], sibling),
            remote(sq_out.at[1], sq_in.at[1], tail_send.at[2], tail_recv.at[2], sibling),
            remote(
                acc.at[3, pl.ds(2 * other, 2)], swap_in.at[3], tail_send.at[3], tail_recv.at[3],
                sibling),
        ]
        swaps[0].start()
        swaps[1].start()

    if RUN_XY:
        xy_sent()
    if RUN_RING:
        for n in range(RING - CHUNKS):
            ring_sent(n)
        for n in range(28, RING):
            ring_round(n)

    if RUN_MATH:
        multiply(3, 0)
        sq_out[1] = jnp.broadcast_to(to_lanes(colsq[3]), (8, 128))
        swaps[2].start()
        swaps[3].start()
        swaps[0].wait()
        scales = lax.rsqrt(sq_out[0] + sq_in[0] + 1e-6)
        swaps[1].wait()
        row_scale = [
            to_rows(jnp.where(c == 0, scales[4 + yy:5 + yy], scales[6 + yy:7 + yy]))
            for yy in range(2)
        ]
        row_here = jnp.where(big_y == 0, row_scale[0], row_scale[1])
        row_there = jnp.where(big_y == 0, row_scale[1], row_scale[0])

        def result(b, yy, row_side, col_side):
            raw = acc[b, 2 * c + yy] + swap_in[b, yy]
            value = raw * row_side * (col_side * math.sqrt(8192.0))
            return jnp.where((row_side > 0.0) & (col_side > 0.0), value, 0.0)

        for b in range(3):
            half_out[b] = result(b, 1 - big_y, row_there, scales[b:b + 1]).astype(jnp.bfloat16)
        across = [
            remote(
                half_out.at[pl.ds(0, 3)], half_in.at[pl.ds(0, 3)], tail_send.at[4],
                tail_recv.at[4], opposite),
            remote(half_out.at[3], half_in.at[3], tail_send.at[5], tail_recv.at[5], opposite),
        ]
        across[0].start()
        swaps[2].wait()
        scale = lax.rsqrt(sq_out[1] + sq_in[1] + 1e-6)[:1]
        swaps[3].wait()
        half_out[3] = result(3, 1 - big_y, row_there, scale).astype(jnp.bfloat16)
        across[1].start()

        def store(b, yy, value):
            at = pl.multiple_of((2 * cube(b) + yy) * 128, 128)
            out_ref[0, :, pl.ds(at, 128)] = value

        for b in range(4):
            value = result(b, big_y, row_here, scales[b:b + 1] if b < 3 else scale)
            if b == 0:
                value = jnp.where(eye & (2 * l + c == ex % 8), 0.0, value)
            store(b, big_y, value)
        across[0].wait()
        for b in range(3):
            store(b, 1 - big_y, half_in[b].astype(jnp.float32))
        across[1].wait()
        store(3, 1 - big_y, half_in[3].astype(jnp.float32))
    else:
        out_ref[...] = jnp.zeros_like(out_ref)
    if RUN_RING:
        for n in range(RING - CHUNKS, RING):
            ring_sent(n)


def local(grads):
    dma = pltpu.SemaphoreType.DMA
    out = pl.pallas_call(
        kernel,
        out_shape=jax.ShapeDtypeStruct((1, 128, 1024), jnp.float32),
        in_specs=[pl.BlockSpec(memory_space=pl.ANY)],
        out_specs=pl.BlockSpec(memory_space=pltpu.VMEM),
        scratch_shapes=[
            pltpu.VMEM((NZ, CHUNKS, PIECE, WIDTH), jnp.bfloat16),
            pltpu.VMEM((4, 16, PIECE, WIDTH), jnp.bfloat16),
            pltpu.VMEM((4, 4, 128, 128), jnp.float32),
            pltpu.VMEM((4, 128, 128), jnp.float32),
            pltpu.VMEM((4, 128, 128), jnp.float32),
            pltpu.VMEM((2, 8, 128), jnp.float32),
            pltpu.VMEM((2, 8, 128), jnp.float32),
            pltpu.VMEM((4, 2, 128, 128), jnp.float32),
            pltpu.VMEM((4, 128, 128), jnp.bfloat16),
            pltpu.VMEM((4, 128, 128), jnp.bfloat16),
            dma,
            dma((2, RING)),
            dma((2, RING)),
            dma((4, 32)),
            dma((4, 8)),
            dma((6,)),
            dma((6,)),
        ],
        compiler_params=pltpu.CompilerParams(
            collective_id=0, has_side_effects=True, vmem_limit_bytes=32 * 1024 * 1024
        ),
        cost_estimate=pl.CostEstimate(
            flops=2 * 512 * 512 * 4096, bytes_accessed=1 << 20, transcendentals=0),
    )(grads.reshape(CHUNKS, PIECE, WIDTH))
    return out


def solution(mesh):
    return jax.shard_map(
        local,
        mesh=mesh,
        in_specs=(P("ex", "feat"),),
        out_specs=P("ex", "feat", None),
        check_vma=False,
    )
```

time: 322 us -> 72.9 us (0.23)
  waiting for transfers between devices: 249 us -> 0 us
  Pallas kernels: 0 us -> 71 us
  starting transfers between devices: 24.7 us -> 0 us
  blocking collectives: 19.8 us -> 0 us
  between operations: 13.5 us -> 0.01 us
  other arithmetic: 6.59 us -> 0 us
  matrix products: 6.56 us -> 0 us
    psum x1 -> x0, waiting for transfers between devices: 140 us -> none  [local(): total = lax.psum(partial_value, 'feat')]
    ppermute x6 -> x0, waiting for transfers between devices: 110 us -> none  [partner(): return lax.ppermute(value, axis, pairs)]
    pallas_call x0 -> x1, Pallas kernels: none -> 71 us  [local(): pl.pallas_call(kernel, out_shape=jax.ShapeDtypeStruct((1, 128, 1024), jnp...]
    ppermute x6 -> x0, starting transfers between devices: 24.7 us -> none  [partner(): return lax.ppermute(value, axis, pairs)]
    psum x1 -> x0, blocking collectives: 19.8 us -> none  [local(): sumsq = lax.psum(jnp.sum(wide * wide, axis=1, keepdims=True), 'feat')]
    dot_general x1 -> x0, matrix products: 6.56 us -> none  [local(): jnp.einsum('rf,cf->rc', row_panel, col_panel, preferred_element_type=jnp....]
  transfers between devices with their start and end apart: 7 -> 0, of which waited for: 5 -> 0; matrix products, arithmetic and copies ran while one was open for 1% -> 0% of each run, Pallas kernels for 0% -> 0%
where the time goes in v2:
time: 72.9 us; the launch traced here: 72.8 us
  Pallas kernels  71 us (97%)
  local copies, waits for them, and re-layouts  1.75 us (2%)
    pallas_call x1, Pallas kernels, local(): pl.pallas_call(kernel, out_shape=jax.ShapeDtypeStruct((1, 128, 1024), jnp...  71 us
    unnamed x3, local copies, waits for them, and re-layouts  1.75 us

profile of v2, /device:TPU:1, one launch (start us, length us, event | category | flops | bytes accessed | tf_op | source)
XLA Modules:
  0.0 72.8 jit_solution(16912428127617256162)
XLA Ops:
  0.0 0.0 copy-start
  0.0 0.9 %copy-done = bf16[128,1024]{1,0:T(8,128)(2,1)S(1)} copy-done((bf16[128,1024]{1,0:T(8,128)(2,1)S(1)}, bf16[128,1024]{1,0:T(8,128)(2,1)}, u32[]{:S(2)}) %copy-start) | copy-done | bytes 262168
  1.0 71.0 %shard_map.17 = f32[1,128,1024]{2,1,0:T(8,128)S(1)} custom-call(bf16[4,32,1024]{2,1,0:T(8,128)(2,1)S(1)} %bitcast.1), custom_call_target="tpu_custom_call" | custom-call | flops 2147483648 | bytes 1048576 | tf_op jit(solution)/shard_map/pallas_call | solution.py:348
  72.0 0.8 %copy.3 = f32[1,128,1024]{2,1,0:T(8,128)} copy(f32[1,128,1024]{2,1,0:T(8,128)S(1)} %shard_map.17) | data formatting | bytes 1048576
Async XLA Ops:
  0.0 0.9 %copy-start = (bf16[128,1024]{1,0:T(8,128)(2,1)S(1)}, bf16[128,1024]{1,0:T(8,128)(2,1)}, u32[]{:S(2)}) copy-start(bf16[128,1024]{1,0:T(8,128)(2,1)} %param.1) | copy-start | bytes 786436

commit v3 on v2

--- a/solution.py
+++ b/solution.py
@@ -20,41 +20,65 @@
 P_TICKS = (16, 20, 21, 24, 25)
 SQ_TICKS = (13, 17, 22, 26)
 EVENTS = (
-    (51561376, 76382242, 52086690, 75858976, 42126276, 85805126, 42651590, 85281860, 67453349, 68995716, 67978663,
-     68472454, 68520385, 67945088, 69045699, 67421826),
-    (1495976, 11046020, 2021290, 10520710, 449484, 20464768, 974798, 19939458, 1575341, 17056896, 1052079,
-     67387522, 524745, 9735300, 1483, 68454534),
-    (890882, 397000, 367616, 920266, 1921030, 1443500, 1397764, 1966766, 69554183, 36756227, 70079493, 37281347,
-     70621187, 35705607, 71146497, 36230695),
-    (96952326, 20519211, 97477636, 37263657, 98019330, 11080015, 98544640, 36196685, 114558466, 35654927,
-     115081728, 36178189, 121900550, 36701451, 122423812, 37224713),
-    (2625037, 71066629, 2099727, 70541319, 3671561, 70036481, 3146251, 69511171, 3939340, 70029866, 3414030,
-     19796520, 2888712, 71064142, 2363402, 12458572),
-    (115349204, 80483024, 115872470, 79959762, 124788400, 89922228, 125311666, 89398966, 2761392, 73214069,
-     2238130, 72690807, 3812052, 72163441, 3288790, 71640179),
-    (5512569, 15248532, 6035835, 14756948, 4461949, 24667280, 4985215, 24192048, 5470731, 13180942, 5996041,
-     12657676, 4436495, 22620170, 4961805, 22096904),
-    (57680911, 56765965, 58204173, 57289231, 48245771, 49423881, 48769033, 49947147, 48246294, 32908881, 48769556,
-     33335057, 57681426, 31862325, 58204688, 32272149),
-    (7613459, 40903483, 8136721, 24127289, 6562839, 39856991, 7086101, 14692189, 4990233, 5914268, 4464923,
-     5388958, 6040861, 4863640, 5515551, 4338330),
-    (7091223, 5652062, 6565909, 6175390, 8141843, 4601402, 7616529, 5124762, 8141852, 23360664, 7616542, 73691290,
-     7091224, 16039068, 6565914, 74758302),
-    (15902, 14873, 14876, 15899, 13850, 12829, 12824, 13855, 13850, 15643, 12824, 14427, 15902, 13599, 14876, 12351),
+    (874972992, 744686276, 879171396, 740496064, 950478728, 753083084, 954677132, 748892872, 537734985, 10171660,
+     541933389, 14361864, 546180993, 1774852, 550379397, 5965056),
+    (143475139, 759367937, 147673543, 755177733, 68051403, 767764745, 72249807, 763574541, 272459009, 12270920,
+     276657413, 16461132, 280904969, 3874176, 285103373, 8064388),
+    (891823569, 550767628, 896021973, 546577416, 967312857, 542387204, 971511261, 538196992, 80749058, 135794958,
+     76558854, 139985162, 139461130, 77082886, 135270926, 81273090),
+    (489689226, 761479432, 493879438, 757289228, 498085954, 769876224, 502276166, 765686020, 12863323, 768944133,
+     8673119, 764753921, 4482963, 760612877, 292759, 756422665),
+    (6297099, 286266382, 2098703, 290456586, 14693891, 294663174, 10495495, 298853378, 11026511, 297795609,
+     15224907, 293605405, 2646151, 289415185, 6844547, 285224981),
+    (21128032, 7612943, 16937828, 3422731, 29442984, 15993351, 25252780, 11803139, 915411972, 7474694, 919602176,
+     3284482, 974140428, 15805966, 978330632, 11615754),
+    (7890401, 30118098, 3700197, 25919702, 16270825, 21737690, 12080621, 17539294, 288453646, 29064536, 292643850,
+     33254748, 296899590, 20667792, 301089794, 24858004),
+    (161494882, 567289107, 165685094, 563098903, 85989290, 558892315, 90179502, 554702111, 6316562, 558135298,
+     2126358, 553936902, 14696986, 566515722, 10506782, 562317326),
+    (23563276, 22249752, 19373064, 18059548, 31960068, 30646544, 27769856, 26456340, 30256135, 362828945, 26065923,
+     367019157, 21924879, 421557337, 17734667, 425747549),
+    (922768923, 303069926, 926959135, 307260130, 998274579, 311450350, 1002464791, 315640554, 570721375, 16819949,
+     574919771, 21018345, 579118231, 25200357, 583316627, 29398753),
+    (14852111, 296254475, 10661899, 300444687, 6389767, 287857667, 2199555, 292047879, 22040602, 154687788,
+     17842206, 158877992, 30437394, 95975716, 26238998, 100165920),
+    (579899889, 792747234, 584090101, 788548838, 571519481, 801144042, 575709693, 796945646, 114326393, 787849239,
+     110127997, 783659027, 173038513, 779517983, 168840117, 775327771),
+    (31311895, 26512428, 27121683, 30710824, 22997023, 18132004, 18806811, 22330400, 42502435, 316688427, 46700839,
+     312498223, 34122027, 308308003, 38320431, 304117799),
+    (523268266, 251961901, 527458478, 256160297, 531648610, 260342309, 535838822, 264540705, 934304790, 38962724,
+     938494994, 34772512, 993033246, 47293996, 997223450, 43103784),
+    (39365670, 49010725, 35175458, 44812321, 47746094, 40630317, 43555882, 36431913, 319929388, 60552554,
+     324119592, 64742766, 328375332, 52155810, 332565536, 56346022),
+    (31645727, 586181937, 27455515, 581991733, 23183383, 577785145, 18993171, 573594941, 37792304, 577040416,
+     33602100, 572842020, 46172728, 585420840, 41982524, 581222444),
+    (41477172, 41142570, 37286960, 36952366, 49857596, 49539362, 45667384, 45349158, 131119141, 394304675,
+     126920737, 398494887, 189831213, 453033067, 185632809, 457223279),
+    (46327853, 43306044, 42137641, 47504440, 37865509, 34925620, 33675297, 39124016, 59296051, 35712767, 63494455,
+     39911163, 50915643, 44093175, 55114047, 48291571),
+    (56159286, 55894589, 51969074, 51704377, 64539710, 64274997, 60349498, 60084785, 62954534, 186175806, 58756130,
+     190366010, 54574126, 127463734, 50375722, 131653938),
+    (57718831, 602975294, 53520427, 598785082, 66099239, 594578486, 61900835, 590388274, 60871807, 50718773,
+     65062011, 54917169, 52491447, 59164733, 56681651, 63363129),
+    (66121789, 59825466, 61923385, 64015678, 57724981, 51445042, 53526577, 55635254, 57735220, 58251443, 53536816,
+     54053047, 66115644, 66648187, 61917240, 62449791),
+    (62, 59, 58, 63, 54, 51, 50, 55, 54, 50, 50, 54, 62, 58, 58, 62),
 )
 DONE = (
-    (101462146, 50864128, 101462146, 50864128, 101462146, 50864128, 101462146, 50864128, 17043456, 0, 17043456, 0,
-     17043456, 0, 17043456, 0),
-    (238068167, 203718981, 238068167, 203718981, 238068167, 203718981, 238068167, 203718981, 136069315, 152846531,
-     136069315, 152846531, 136069315, 152846531, 136069315, 152846531),
-    (391464015, 340857869, 391464015, 340857869, 391464015, 340857869, 391464015, 340857869, 289469195, 305984203,
-     289469195, 305984203, 289469195, 305984203, 289469195, 305984203),
-    (494253720, 510772760, 494253720, 510772760, 494253720, 510772760, 494253720, 510772760, 459638100, 459634003,
-     459638100, 459634003, 459638100, 459634003, 459638100, 459634003),
-    (545392607, 545388510, 545392607, 545388510, 545392607, 545388510, 545392607, 545388510, 545384348, 545388509,
-     545384348, 545388509, 545384348, 545388509, 545384348, 545388509),
-    (133152, 133152, 133152, 133152, 133152, 133152, 133152, 133152, 133152, 133152, 133152, 133152, 133152,
-     133152, 133152, 133152),
+    (21103364, 10551552, 21103364, 10551552, 21103364, 10551552, 21103364, 10551552, 4227200, 0, 4227200, 0,
+     4227200, 0, 4227200, 0),
+    (50661517, 40093064, 50661517, 40093064, 50661517, 40093064, 50661517, 40093064, 27411204, 29524739, 27411204,
+     29524739, 27411204, 29524739, 27411204, 29524739),
+    (84480028, 71798038, 84480028, 71798038, 84480028, 71798038, 84480028, 71798038, 57002384, 63343378, 57002384,
+     63343378, 57002384, 63343378, 57002384, 63343378),
+    (111974316, 105616678, 111974316, 105616678, 111974316, 105616678, 111974316, 105616678, 90821023, 97162018,
+     90821023, 97162018, 90821023, 97162018, 90821023, 97162018),
+    (128900408, 128883765, 128900408, 128883765, 128900408, 128883765, 128900408, 128883765, 120428847, 126786354,
+     120428847, 126786354, 120428847, 126786354, 120428847, 126786354),
+    (135274558, 135258046, 135274558, 135258046, 135274558, 135258046, 135274558, 135258046, 135257916, 135274559,
+     135257916, 135274559, 135257916, 135274559, 135257916, 135274559),
+    (135274560, 135274560, 135274560, 135274560, 135274560, 135274560, 135274560, 135274560, 135274560, 135274560,
+     135274560, 135274560, 135274560, 135274560, 135274560, 135274560),
 )
 
 
@@ -130,34 +154,34 @@
 
     events = [here(table) for table in EVENTS]
     done = [here(table) for table in DONE]
-    handled = [jnp.int32(0)] + [done[n // 5] // 64 ** (n % 5) % 64 for n in range(28)]
+    handled = [jnp.int32(0)] + [done[n // 4] // 128 ** (n % 4) % 128 for n in range(28)]
 
     def slice_of(k):
         return (l // 2 + k // 2) % 2 * 2 + (l + k) % 2
 
-    def own_copy(k, part):
-        q = 2 * (2 * dx + dy // 2) + part
-        return pltpu.make_async_copy(
-            cols.at[h * 4 + slice_of(k), pl.ds(2 * part, 2)],
-            rows.at[slice_of(k), pl.ds(2 * q, 2)], xy_recv.at[k, q],
-        )
-
-    def set_out(k):
+    def row_piece(k, q):
+        part = q % 4
+        part = jnp.where(slice_of(k) > l, 3 - part, part)
+        return rows.at[slice_of(k), q // 4 * 4 + part]
+
+    def set_out(k, part):
         @pl.when(source)
         def _():
-            for part in range(2):
-                own_copy(k, part).start()
+            q = 4 * (2 * dx + dy // 2) + part
+            chunk = jnp.where(slice_of(k) > l, 3 - part, part)
+            pltpu.make_async_copy(
+                cols.at[h * 4 + slice_of(k), chunk], row_piece(k, q), xy_recv.at[k, q]).start()
 
     def decoded(e):
         third = e // 3
         word = events[0]
         for index in range(1, len(events)):
             word = jnp.where(third == index, events[index], word)
-        digit = jnp.right_shift(word, (e - third * 3) * 9)
-        return digit // 8 % 4, digit % 8, [digit // (32 * 2**d) % 2 == 1 for d in range(4)]
+        digit = jnp.right_shift(word, (e - third * 3) * 10)
+        return digit // 16 % 4, digit % 16, [digit // (64 * 2**d) % 2 == 1 for d in range(4)]
 
     def onward(k, q, d):
-        ref = rows.at[slice_of(k), pl.ds(2 * q, 2)]
+        ref = row_piece(k, q)
         return remote(ref, ref, xy_send.at[k, 4 * q + d], xy_recv.at[k, q], plane[d])
 
     def take(e, carry):
@@ -170,14 +194,14 @@
     def take_until(n):
         lax.fori_loop(handled[n], handled[n + 1], take, 0)
 
-    def xy_sent():
+    def xy_sent(start, stop):
         def body(e, carry):
             k, q, goes = decoded(e)
             for d in range(4):
                 pl.when(goes[d])(onward(k, q, d).wait_send)
             return carry
 
-        lax.fori_loop(0, 32, body, 0)
+        lax.fori_loop(start, stop, body, 0)
 
     def squares(block):
         wide = block.astype(jnp.float32)
@@ -247,8 +271,11 @@
             ring_start(n)
     for tick in range(28):
         if RUN_XY:
-            if tick % CHUNKS == 0 and tick < 4 * CHUNKS:
-                set_out(tick // CHUNKS)
+            if tick == 0:
+                for part in range(4):
+                    set_out(0, part)
+            elif tick <= 3 * CHUNKS:
+                set_out(1 + (tick - 1) // CHUNKS, (tick - 1) % CHUNKS)
             take_until(tick)
         if RUN_MATH:
             if tick in SQ_TICKS:
@@ -257,6 +284,17 @@
                 plan[tick]()
         if RUN_RING:
             ring_round(tick)
+            if tick >= 8:
+                ring_sent(tick - 8)
+        if RUN_XY and tick >= 16:
+            xy_sent(handled[tick - 8] if tick > 16 else 0, handled[tick - 7])
+
+    def settle():
+        if RUN_XY:
+            xy_sent(handled[20], 64)
+        if RUN_RING:
+            for n in range(20, RING):
+                ring_sent(n)
 
     other = 1 - c
     if RUN_MATH:
@@ -279,11 +317,7 @@
         swaps[0].start()
         swaps[1].start()
 
-    if RUN_XY:
-        xy_sent()
     if RUN_RING:
-        for n in range(RING - CHUNKS):
-            ring_sent(n)
         for n in range(28, RING):
             ring_round(n)
 
@@ -331,6 +365,7 @@
             if b == 0:
                 value = jnp.where(eye & (2 * l + c == ex % 8), 0.0, value)
             store(b, big_y, value)
+        settle()
         across[0].wait()
         for b in range(3):
             store(b, 1 - big_y, half_in[b].astype(jnp.float32))
@@ -338,9 +373,7 @@
         store(3, 1 - big_y, half_in[3].astype(jnp.float32))
     else:
         out_ref[...] = jnp.zeros_like(out_ref)
-    if RUN_RING:
-        for n in range(RING - CHUNKS, RING):
-            ring_sent(n)
+        settle()
 
 
 def local(grads):
@@ -364,8 +397,8 @@
             dma,
             dma((2, RING)),
             dma((2, RING)),
-            dma((4, 32)),
-            dma((4, 8)),
+            dma((4, 64)),
+            dma((4, 16)),
             dma((6,)),
             dma((6,)),
         ],
@@ -374,7 +407,7 @@
         ),
         cost_estimate=pl.CostEstimate(
             flops=2 * 512 * 512 * 4096, bytes_accessed=1 << 20, transcendentals=0),
-    )(grads.reshape(CHUNKS, PIECE, WIDTH))
+    )(pltpu.with_memory_space_constraint(grads.reshape(CHUNKS, PIECE, WIDTH), pltpu.HBM))
     return out
 
 

time: 72.9 us -> 69.9 us (0.959)
  Pallas kernels: 71 us -> 69 us
  local copies, waits for them, and re-layouts: 1.75 us -> 0.8 us
    pallas_call x1, Pallas kernels: 71 us -> 69 us  [local(): pl.pallas_call(kernel, out_shape=jax.ShapeDtypeStruct((1, 128, 1024), jnp...]
    unnamed x3 -> x1, local copies, waits for them, and re-layouts: 1.75 us -> 0.8 us
where the time goes in v3:
time: 69.9 us; the launch traced here: 69.8 us
  Pallas kernels  69 us (99%)
  local copies, waits for them, and re-layouts  0.8 us (1%)
    pallas_call x1, Pallas kernels, local(): pl.pallas_call(kernel, out_shape=jax.ShapeDtypeStruct((1, 128, 1024), jnp...  69 us

profile of v3, /device:TPU:1, one launch (start us, length us, event | category | flops | bytes accessed | tf_op | source)
XLA Modules:
  0.0 69.8 jit_solution(826506307254786698)
XLA Ops:
  0.0 69.0 %shard_map.17 = f32[1,128,1024]{2,1,0:T(8,128)S(1)} custom-call(bf16[4,32,1024]{2,1,0:T(8,128)(2,1)} %bitcast.1), custom_call_target="tpu_custom_call" | custom-call | flops 2147483648 | bytes 1048576 | tf_op jit(solution)/shard_map/pallas_call | solution.py:381
  69.0 0.8 %copy.3 = f32[1,128,1024]{2,1,0:T(8,128)} copy(f32[1,128,1024]{2,1,0:T(8,128)S(1)} %shard_map.17) | data formatting | bytes 1048576

commit v4 on v3

--- a/solution.py
+++ b/solution.py
@@ -14,11 +14,6 @@
 CHUNKS = 4
 PIECE = 32
 RING = 30
-RUN_RING = True
-RUN_XY = True
-RUN_MATH = True
-P_TICKS = (16, 20, 21, 24, 25)
-SQ_TICKS = (13, 17, 22, 26)
 EVENTS = (
     (874972992, 744686276, 879171396, 740496064, 950478728, 753083084, 954677132, 748892872, 537734985, 10171660,
      541933389, 14361864, 546180993, 1774852, 550379397, 5965056),
@@ -119,6 +114,19 @@
         pl.semaphore_signal(barrier, inc=1, device_id=to, device_id_type=MESH)
     acc[...] = jnp.zeros_like(acc)
     colsq[...] = jnp.zeros_like(colsq)
+    place = dx * 4 + dy
+    source = (dx < 2) & (dy % 2 == 0)
+
+    def here(table):
+        value = jnp.int32(table[0])
+        for index, entry in enumerate(table[1:], 1):
+            value = jnp.where(place == index, jnp.int32(entry), value)
+        return value
+
+    events = [here(table) for table in EVENTS]
+    done = [here(table) for table in DONE]
+    handled = [jnp.int32(0)] + [done[n // 4] // 128 ** (n % 4) % 128 for n in range(28)]
+
     load.wait()
     pl.semaphore_wait(barrier, 8)
 
@@ -143,18 +151,8 @@
         for way in range(2):
             ring_copy(way, n, 0).wait_send()
 
-    place = dx * 4 + dy
-    source = (dx < 2) & (dy % 2 == 0)
-
-    def here(table):
-        value = jnp.int32(table[0])
-        for index, entry in enumerate(table[1:], 1):
-            value = jnp.where(place == index, jnp.int32(entry), value)
-        return value
-
-    events = [here(table) for table in EVENTS]
-    done = [here(table) for table in DONE]
-    handled = [jnp.int32(0)] + [done[n // 4] // 128 ** (n % 4) % 128 for n in range(28)]
+    for n in range(CHUNKS):
+        ring_start(n)
 
     def slice_of(k):
         return (l // 2 + k // 2) % 2 * 2 + (l + k) % 2
@@ -224,16 +222,6 @@
         acc[b] += product.reshape(4, ROWS, 128)
         colsq[b] += squares(block)
 
-    def multiply_all(k, blocks):
-        def body(i, carry):
-            b = blocks[0]
-            for index in range(1, len(blocks)):
-                b = jnp.where(i == index, blocks[index], b)
-            multiply(b % 4, k)
-            return carry
-
-        lax.fori_loop(0, len(blocks), body, 0)
-
     def row_squares(k):
         ll = slice_of(k)
 
@@ -259,123 +247,107 @@
     last = jnp.where(l == 0, 1, jnp.where(l == 3, 2, 3))
 
     far = jnp.where(l < 2, 1, 2)
-    plan = {
-        P_TICKS[0]: lambda: multiply_all(0, (0, 1, 2)),
-        P_TICKS[1]: lambda: multiply_all(1, (0, 1, 2)),
-        P_TICKS[2]: lambda: multiply_all(2, (0, 3 - far)),
-        P_TICKS[3]: lambda: multiply_all(2, (far, 3)),
-        P_TICKS[4]: lambda: multiply_all(3, (last + 1, last + 2, last + 3)),
+    near = 3 - far
+    products = {
+        12: [(0, 0)], 16: [(1, 0)], 17: [(2, 0)], 18: [(0, 1)], 20: [(1, 1)], 21: [(2, 1)], 22: [(0, 2)],
+        23: [(near, 2)], 24: [(far, 2)], 25: [(3, 2)],
+        26: [((last + 1) % 4, 3), ((last + 2) % 4, 3), ((last + 3) % 4, 3)],
     }
-    if RUN_RING:
-        for n in range(CHUNKS):
-            ring_start(n)
+    row_sums = {13: 0, 19: 1, 24: 2, 26: 3}
     for tick in range(28):
-        if RUN_XY:
-            if tick == 0:
-                for part in range(4):
-                    set_out(0, part)
-            elif tick <= 3 * CHUNKS:
-                set_out(1 + (tick - 1) // CHUNKS, (tick - 1) % CHUNKS)
-            take_until(tick)
-        if RUN_MATH:
-            if tick in SQ_TICKS:
-                row_squares(SQ_TICKS.index(tick))
-            if tick in plan:
-                plan[tick]()
-        if RUN_RING:
-            ring_round(tick)
-            if tick >= 8:
-                ring_sent(tick - 8)
-        if RUN_XY and tick >= 16:
+        if tick == 0:
+            for part in range(4):
+                set_out(0, part)
+        elif tick <= 3 * CHUNKS:
+            set_out(1 + (tick - 1) // CHUNKS, (tick - 1) % CHUNKS)
+        take_until(tick)
+        if tick in row_sums:
+            row_squares(row_sums[tick])
+        for b, k in products.get(tick, ()):
+            multiply(b, k)
+        ring_round(tick)
+        if tick >= 8:
+            ring_sent(tick - 8)
+        if tick >= 16:
             xy_sent(handled[tick - 8] if tick > 16 else 0, handled[tick - 7])
 
     def settle():
-        if RUN_XY:
-            xy_sent(handled[20], 64)
-        if RUN_RING:
-            for n in range(20, RING):
-                ring_sent(n)
+        xy_sent(handled[20], 64)
+        for n in range(20, RING):
+            ring_sent(n)
 
     other = 1 - c
-    if RUN_MATH:
-        multiply(3, 1)
-        multiply(last, 3)
-        for b in range(3):
-            sq_out[0, b:b + 1] = to_lanes(colsq[b])
-        for p in range(4):
-            sq_out[0, 4 + p:5 + p] = to_lanes(rowsq[p])
-        swaps = [
-            remote(sq_out.at[0], sq_in.at[0], tail_send.at[0], tail_recv.at[0], sibling),
-            remote(
-                acc.at[pl.ds(0, 3), pl.ds(2 * other, 2)], swap_in.at[pl.ds(0, 3)], tail_send.at[1],
-                tail_recv.at[1], sibling),
-            remote(sq_out.at[1], sq_in.at[1], tail_send.at[2], tail_recv.at[2], sibling),
-            remote(
-                acc.at[3, pl.ds(2 * other, 2)], swap_in.at[3], tail_send.at[3], tail_recv.at[3],
-                sibling),
-        ]
-        swaps[0].start()
-        swaps[1].start()
-
-    if RUN_RING:
-        for n in range(28, RING):
-            ring_round(n)
-
-    if RUN_MATH:
-        multiply(3, 0)
-        sq_out[1] = jnp.broadcast_to(to_lanes(colsq[3]), (8, 128))
-        swaps[2].start()
-        swaps[3].start()
-        swaps[0].wait()
-        scales = lax.rsqrt(sq_out[0] + sq_in[0] + 1e-6)
-        swaps[1].wait()
-        row_scale = [
-            to_rows(jnp.where(c == 0, scales[4 + yy:5 + yy], scales[6 + yy:7 + yy]))
-            for yy in range(2)
-        ]
-        row_here = jnp.where(big_y == 0, row_scale[0], row_scale[1])
-        row_there = jnp.where(big_y == 0, row_scale[1], row_scale[0])
-
-        def result(b, yy, row_side, col_side):
-            raw = acc[b, 2 * c + yy] + swap_in[b, yy]
-            value = raw * row_side * (col_side * math.sqrt(8192.0))
-            return jnp.where((row_side > 0.0) & (col_side > 0.0), value, 0.0)
-
-        for b in range(3):
-            half_out[b] = result(b, 1 - big_y, row_there, scales[b:b + 1]).astype(jnp.bfloat16)
-        across = [
-            remote(
-                half_out.at[pl.ds(0, 3)], half_in.at[pl.ds(0, 3)], tail_send.at[4],
-                tail_recv.at[4], opposite),
-            remote(half_out.at[3], half_in.at[3], tail_send.at[5], tail_recv.at[5], opposite),
-        ]
-        across[0].start()
-        swaps[2].wait()
-        scale = lax.rsqrt(sq_out[1] + sq_in[1] + 1e-6)[:1]
-        swaps[3].wait()
-        half_out[3] = result(3, 1 - big_y, row_there, scale).astype(jnp.bfloat16)
-        across[1].start()
-
-        def store(b, yy, value):
-            at = pl.multiple_of((2 * cube(b) + yy) * 128, 128)
-            out_ref[0, :, pl.ds(at, 128)] = value
-
-        for b in range(4):
-            value = result(b, big_y, row_here, scales[b:b + 1] if b < 3 else scale)
-            if b == 0:
-                value = jnp.where(eye & (2 * l + c == ex % 8), 0.0, value)
-            store(b, big_y, value)
-        settle()
-        across[0].wait()
-        for b in range(3):
-            store(b, 1 - big_y, half_in[b].astype(jnp.float32))
-        across[1].wait()
-        store(3, 1 - big_y, half_in[3].astype(jnp.float32))
-    else:
-        out_ref[...] = jnp.zeros_like(out_ref)
-        settle()
-
-
+    multiply(3, 1)
+    multiply(last, 3)
+    for b in range(3):
+        sq_out[0, b:b + 1] = to_lanes(colsq[b])
+    for p in range(4):
+        sq_out[0, 4 + p:5 + p] = to_lanes(rowsq[p])
+    swaps = [
+        remote(sq_out.at[0], sq_in.at[0], tail_send.at[0], tail_recv.at[0], sibling),
+        remote(
+            acc.at[pl.ds(0, 3), pl.ds(2 * other, 2)], swap_in.at[pl.ds(0, 3)], tail_send.at[1],
+            tail_recv.at[1], sibling),
+        remote(sq_out.at[1], sq_in.at[1], tail_send.at[2], tail_recv.at[2], sibling),
+        remote(
+            acc.at[3, pl.ds(2 * other, 2)], swap_in.at[3], tail_send.at[3], tail_recv.at[3],
+            sibling),
+    ]
+    swaps[0].start()
+    swaps[1].start()
+
+    for n in range(28, RING):
+        ring_round(n)
+
+    multiply(3, 0)
+    sq_out[1] = jnp.broadcast_to(to_lanes(colsq[3]), (8, 128))
+    swaps[2].start()
+    swaps[3].start()
+    swaps[0].wait()
+    scales = lax.rsqrt(sq_out[0] + sq_in[0] + 1e-6)
+    swaps[1].wait()
+    row_scale = [
+        to_rows(jnp.where(c == 0, scales[4 + yy:5 + yy], scales[6 + yy:7 + yy]))
+        for yy in range(2)
+    ]
+    row_here = jnp.where(big_y == 0, row_scale[0], row_scale[1])
+    row_there = jnp.where(big_y == 0, row_scale[1], row_scale[0])
+
+    def result(b, yy, row_side, col_side):
+        raw = acc[b, 2 * c + yy] + swap_in[b, yy]
+        value = raw * row_side * (col_side * math.sqrt(8192.0))
+        return jnp.where((row_side > 0.0) & (col_side > 0.0), value, 0.0)
+
+    for b in range(3):
+        half_out[b] = result(b, 1 - big_y, row_there, scales[b:b + 1]).astype(jnp.bfloat16)
+    across = [
+        remote(
+            half_out.at[pl.ds(0, 3)], half_in.at[pl.ds(0, 3)], tail_send.at[4],
+            tail_recv.at[4], opposite),
+        remote(half_out.at[3], half_in.at[3], tail_send.at[5], tail_recv.at[5], opposite),
+    ]
+    across[0].start()
+    swaps[2].wait()
+    scale = lax.rsqrt(sq_out[1] + sq_in[1] + 1e-6)[:1]
+    swaps[3].wait()
+    half_out[3] = result(3, 1 - big_y, row_there, scale).astype(jnp.bfloat16)
+    across[1].start()
+
+    def store(b, yy, value):
+        at = pl.multiple_of((2 * cube(b) + yy) * 128, 128)
+        out_ref[0, :, pl.ds(at, 128)] = value
+
+    for b in range(4):
+        value = result(b, big_y, row_here, scales[b:b + 1] if b < 3 else scale)
+        if b == 0:
+            value = jnp.where(eye & (2 * l + c == ex % 8), 0.0, value)
+        store(b, big_y, value)
+    settle()
+    across[0].wait()
+    for b in range(3):
+        store(b, 1 - big_y, half_in[b].astype(jnp.float32))
+    across[1].wait()
+    store(3, 1 - big_y, half_in[3].astype(jnp.float32))
 def local(grads):
     dma = pltpu.SemaphoreType.DMA
     out = pl.pallas_call(

time: 69.9 us -> 69.2 us (0.990)
  Pallas kernels: 69 us -> 68.2 us
    pallas_call x1, Pallas kernels: 69 us -> 68.2 us  [local(): pl.pallas_call(kernel, out_shape=jax.ShapeDtypeStruct((1, 128, 1024), jnp...]
where the time goes in v4:
time: 69.2 us; the launch traced here: 69 us
  Pallas kernels  68.2 us (99%)
  local copies, waits for them, and re-layouts  0.8 us (1%)
    pallas_call x1, Pallas kernels, local(): pl.pallas_call(kernel, out_shape=jax.ShapeDtypeStruct((1, 128, 1024), jnp...  68.2 us

profile of v4, /device:TPU:1, one launch (start us, length us, event | category | flops | bytes accessed | tf_op | source)
XLA Modules:
  0.0 69.0 jit_solution(15154578588401163673)
XLA Ops:
  0.0 68.2 %shard_map.17 = f32[1,128,1024]{2,1,0:T(8,128)S(1)} custom-call(bf16[4,32,1024]{2,1,0:T(8,128)(2,1)} %bitcast.1), custom_call_target="tpu_custom_call" | custom-call | flops 2147483648 | bytes 1048576 | tf_op jit(solution)/shard_map/pallas_call | solution.py:353
  68.2 0.8 %copy.3 = f32[1,128,1024]{2,1,0:T(8,128)} copy(f32[1,128,1024]{2,1,0:T(8,128)S(1)} %shard_map.17) | data formatting | bytes 1048576

commit v5 on v4

--- a/solution.py
+++ b/solution.py
@@ -112,21 +112,6 @@
     barrier = pltpu.get_barrier_semaphore()
     for to in (z_up, z_down, *plane, opposite, sibling):
         pl.semaphore_signal(barrier, inc=1, device_id=to, device_id_type=MESH)
-    acc[...] = jnp.zeros_like(acc)
-    colsq[...] = jnp.zeros_like(colsq)
-    place = dx * 4 + dy
-    source = (dx < 2) & (dy % 2 == 0)
-
-    def here(table):
-        value = jnp.int32(table[0])
-        for index, entry in enumerate(table[1:], 1):
-            value = jnp.where(place == index, jnp.int32(entry), value)
-        return value
-
-    events = [here(table) for table in EVENTS]
-    done = [here(table) for table in DONE]
-    handled = [jnp.int32(0)] + [done[n // 4] // 128 ** (n % 4) % 128 for n in range(28)]
-
     load.wait()
     pl.semaphore_wait(barrier, 8)
 
@@ -153,6 +138,19 @@
 
     for n in range(CHUNKS):
         ring_start(n)
+
+    place = dx * 4 + dy
+    source = (dx < 2) & (dy % 2 == 0)
+
+    def here(table):
+        value = jnp.int32(table[0])
+        for index, entry in enumerate(table[1:], 1):
+            value = jnp.where(place == index, jnp.int32(entry), value)
+        return value
+
+    events = [here(table) for table in EVENTS]
+    done = [here(table) for table in DONE]
+    handled = [jnp.int32(0)] + [done[n // 4] // 128 ** (n % 4) % 128 for n in range(28)]
 
     def slice_of(k):
         return (l // 2 + k // 2) % 2 * 2 + (l + k) % 2
@@ -246,6 +244,10 @@
 
     last = jnp.where(l == 0, 1, jnp.where(l == 3, 2, 3))
 
+    for part in range(4):
+        set_out(0, part)
+    acc[...] = jnp.zeros_like(acc)
+    colsq[...] = jnp.zeros_like(colsq)
     far = jnp.where(l < 2, 1, 2)
     near = 3 - far
     products = {
@@ -255,10 +257,7 @@
     }
     row_sums = {13: 0, 19: 1, 24: 2, 26: 3}
     for tick in range(28):
-        if tick == 0:
-            for part in range(4):
-                set_out(0, part)
-        elif tick <= 3 * CHUNKS:
+        if 0 < tick <= 3 * CHUNKS:
             set_out(1 + (tick - 1) // CHUNKS, (tick - 1) % CHUNKS)
         take_until(tick)
         if tick in row_sums:

time: 69.2 us -> 69 us (level)
  no operation moved by 1% of the time
where the time goes in v5:
time: 69 us; the launch traced here: 68.9 us
  Pallas kernels  68.1 us (99%)
  local copies, waits for them, and re-layouts  0.8 us (1%)
    pallas_call x1, Pallas kernels, local(): pl.pallas_call(kernel, out_shape=jax.ShapeDtypeStruct((1, 128, 1024), jnp...  68.1 us

profile of v5, /device:TPU:1, one launch (start us, length us, event | category | flops | bytes accessed | tf_op | source)
XLA Modules:
  0.0 68.9 jit_solution(9755683470928159066)
XLA Ops:
  0.0 68.1 %shard_map.17 = f32[1,128,1024]{2,1,0:T(8,128)S(1)} custom-call(bf16[4,32,1024]{2,1,0:T(8,128)(2,1)} %bitcast.1), custom_call_target="tpu_custom_call" | custom-call | flops 2147483648 | bytes 1048576 | tf_op jit(solution)/shard_map/pallas_call | solution.py:352
  68.1 0.8 %copy.3 = f32[1,128,1024]{2,1,0:T(8,128)} copy(f32[1,128,1024]{2,1,0:T(8,128)S(1)} %shard_map.17) | data formatting | bytes 1048576
